TPU v7x, 512 devices: a whole 4x4x16 slice. The times are simulated.
512 devices in a mesh: ctx: 64 (over z_hi, y, x, core), head: 8 (over z_lo).
Axes of the slice: x: 4, y: 4, z: 16 (z_hi: 2, z_lo: 8; z = z_hi * 8 + z_lo), core: 2. Of those that a mesh axis runs over, the one named last changes fastest.
Arguments:
- queries: bfloat16 [32768, 5120], P(('ctx', 'head')), may hold values from -6 to 6
- keys: bfloat16 [32768, 5120], P(('ctx', 'head')), may hold values from -6 to 6
- values: bfloat16 [32768, 5120], P(('ctx', 'head')), may hold values from -6 to 6
- grad_out: bfloat16 [32768, 5120], P(('ctx', 'head')), may hold values from -150 to 150
- neighbours: int32 [512, 16], replicated, may hold values from 0 to 511, as said below
- counts: int32 [512], replicated, may hold values from 1 to 16, as said below
Outputs:
- grad_queries: bfloat16 [32768, 5120], P(('ctx', 'head'))
- grad_keys: bfloat16 [32768, 5120], P(('ctx', 'head'))
- grad_values: bfloat16 [32768, 5120], P(('ctx', 'head'))
Inputs may be any that keep to these rules, and one draw needn't show every extreme that they name: `neighbours`: row t holds 16 distinct tile numbers; the first is t itself; each lies in t's slab of 8 tiles (tiles s * 8 to s * 8 + 7) or within the 8 tiles of the slabs beside it that are nearest to it. For the first tile of a slab that is not the first slab, the second entry is the tile just below it; for the last tile of a slab that is not the last slab, the second entry is the tile just above it. `counts`: the first tile of every slab uses all 16 entries; the last tile of every slab uses 2 or more.
All inputs are finite; a program needn't handle non-finite values.
Results may differ from a plain program's by a relative error of at most 0.0095.
Values may be sent and summed in bfloat16 or wider, within the bound.
A program may use at most 128 MiB of HBM per device.

v0:
```python
import math

import jax
import jax.numpy as jnp
from jax import lax
from jax.sharding import PartitionSpec as P

DH = 128
TILE = 64
HALO_TILES = 8
TILES_DEV = 8


def extended(block, sides, width):
    for axis, dim in sides:
        count = lax.axis_size(axis)
        forward = [(i, i + 1) for i in range(count - 1)]
        backward = [(target, source) for source, target in forward]
        low = lax.ppermute(
            lax.slice_in_dim(block, block.shape[dim] - width, None, axis=dim), axis, forward
        )
        high = lax.ppermute(lax.slice_in_dim(block, 0, width, axis=dim), axis, backward)
        block = jnp.concatenate([low, block, high], axis=dim)
    return block


def passed_along(array, axis, by):
    devices = lax.axis_size(axis)
    pairs = [(i, i + by) for i in range(devices) if 0 <= i + by < devices]
    return lax.ppermute(array, axis, pairs)


def split_heads(array, head_count):
    return array.reshape(array.shape[0], head_count, DH).transpose(1, 0, 2)


def join_heads(array):
    return array.transpose(1, 0, 2).reshape(array.shape[1], array.shape[0] * array.shape[2])


def tile_mask(rows_nbr, rows_cnt, first_id, ncols):
    relative = rows_nbr - first_id
    listed = lax.broadcasted_iota(jnp.int32, rows_nbr.shape, 1) < rows_cnt[:, None]
    columns = lax.broadcasted_iota(jnp.int32, (1, 1, ncols), 2)
    permitted = jnp.any((relative[:, :, None] == columns) & listed[:, :, None], axis=1) & True
    return jnp.repeat(jnp.repeat(permitted, TILE, axis=0), TILE, axis=1)


def attend(query_h, key_h, value_h, cotan_h, permitted):
    scale = 1.0 / math.sqrt(DH)
    scores = jnp.einsum("rd,wd->rw", query_h, key_h, preferred_element_type=jnp.float32) * scale
    top_score = jnp.max(jnp.where(permitted, scores, -jnp.inf), axis=1, keepdims=True)
    expo = jnp.where(permitted, jnp.exp(scores - top_score), 0.0)
    total_sum = jnp.sum(expo, axis=1, keepdims=True)
    probs = expo / total_sum
    probs_b = probs.astype(jnp.bfloat16)
    output = jnp.dot(probs_b, value_h, preferred_element_type=jnp.float32)
    delta = jnp.sum(cotan_h.astype(jnp.float32) * output, axis=1, keepdims=True)
    grad_p = jnp.einsum("rd,wd->rw", cotan_h, value_h, preferred_element_type=jnp.float32)
    grad_sb = (probs * (grad_p - delta)).astype(jnp.bfloat16)
    grad_q = jnp.dot(grad_sb, key_h, preferred_element_type=jnp.float32) * scale
    part_k = jnp.einsum("rw,rd->wd", grad_sb, query_h, preferred_element_type=jnp.float32) * scale
    part_v = jnp.einsum("rw,rd->wd", probs_b, cotan_h, preferred_element_type=jnp.float32)
    return (grad_q, part_k, part_v, top_score[:, 0], total_sum[:, 0], delta[:, 0])


def per_device(queries, keys, values, grad_out, neighbours, counts):
    query_rows, key_rows, value_rows, cotan_rows = (
        lax.all_to_all(queries, "head", split_axis=1, concat_axis=0, tiled=True),
        lax.all_to_all(keys, "head", split_axis=1, concat_axis=0, tiled=True),
        lax.all_to_all(values, "head", split_axis=1, concat_axis=0, tiled=True),
        lax.all_to_all(grad_out, "head", split_axis=1, concat_axis=0, tiled=True),
    )
    head_count = query_rows.shape[1] // DH
    row_count = query_rows.shape[0]
    reach_rows = HALO_TILES * TILE
    query_heads = split_heads(query_rows, head_count)
    cotan_heads = split_heads(cotan_rows, head_count)
    paired = jnp.stack([split_heads(key_rows, head_count), split_heads(value_rows, head_count)])
    window_kv = extended(paired, (("ctx", 2),), reach_rows)
    slab_index = lax.axis_index("ctx")
    first_tile = slab_index * TILES_DEV
    own_nbr = lax.dynamic_slice_in_dim(neighbours, first_tile, TILES_DEV, 0)
    own_cnt = lax.dynamic_slice_in_dim(counts, first_tile, TILES_DEV, 0)
    key_mask = tile_mask(own_nbr, own_cnt, first_tile - HALO_TILES, TILES_DEV + 2 * HALO_TILES)

    def head_pass(items):
        return attend(items[0], items[1], items[2], items[3], key_mask)[:3]

    grad_q, window_k, window_v = lax.map(
        head_pass, (query_heads, window_kv[0], window_kv[1], cotan_heads)
    )
    partials = jnp.stack([window_k, window_v])
    from_above = passed_along(partials[:, :, :reach_rows].astype(jnp.bfloat16), "ctx", -1).astype(
        jnp.float32
    )
    from_below = passed_along(
        partials[:, :, reach_rows + row_count :].astype(jnp.bfloat16), "ctx", 1
    ).astype(jnp.float32)
    own_parts = partials[:, :, reach_rows : reach_rows + row_count]
    own_parts = own_parts.at[:, :, :reach_rows].add(from_below)
    own_parts = own_parts.at[:, :, row_count - reach_rows :].add(from_above)
    grad_q_rows = join_heads(grad_q).astype(jnp.bfloat16)
    grad_k_rows = join_heads(own_parts[0]).astype(jnp.bfloat16)
    grad_v_rows = join_heads(own_parts[1]).astype(jnp.bfloat16)
    grad_queries, grad_keys, grad_values = (
        lax.all_to_all(grad_q_rows, "head", split_axis=0, concat_axis=1, tiled=True),
        lax.all_to_all(grad_k_rows, "head", split_axis=0, concat_axis=1, tiled=True),
        lax.all_to_all(grad_v_rows, "head", split_axis=0, concat_axis=1, tiled=True),
    )
    return (grad_queries, grad_keys, grad_values)


def solution(mesh):
    in_specs = (
        P(("ctx", "head"), None),
        P(("ctx", "head"), None),
        P(("ctx", "head"), None),
        P(("ctx", "head"), None),
        P(),
        P(),
    )
    out_specs = (P(("ctx", "head"), None), P(("ctx", "head"), None), P(("ctx", "head"), None))
    return jax.shard_map(
        per_device, mesh=mesh, in_specs=in_specs, out_specs=out_specs, check_vma=False
    )
```

profile of v0, /device:TPU:63, one launch (start us, length us, event | category | flops | bytes accessed | tf_op | source)
XLA Modules:
  0.0 467.9 jit_solution(1618222391791760211)
XLA Ops:
  2.7 12.1 %all-to-all-start.1 = ((bf16[64,8,640]{2,0,1:T(8,128)(2,1)}), bf16[64,8,640]{2,0,1:T(8,128)(2,1)S(1)}, u32[]{:S(2)}, u32[]{:S(2)}) async-start(bf16[64,8,640]{2,0,1:T(8,128)(2,1)} %bitcast.94), calls=%async_computation.1 | async-start | bytes 1310720 | tf_op jit(solution)/shard_map/all_to_all | solution.py:70
  16.8 29.1 %all-to-all-done.1 = bf16[64,8,640]{2,0,1:T(8,128)(2,1)S(1)} async-done(((bf16[64,8,640]{2,0,1:T(8,128)(2,1)}), bf16[64,8,640]{2,0,1:T(8,128)(2,1)S(1)}, u32[]{:S(2)}, u32[]{:S(2)}) %all-to-all-start.1) | async-done | bytes 655392 | tf_op jit(solution)/shard_map/all_to_all | solution.py:70
  45.9 7.3 %all-to-all-start.2 = ((bf16[64,8,640]{2,0,1:T(8,128)(2,1)}), bf16[64,8,640]{2,0,1:T(8,128)(2,1)S(1)}, u32[]{:S(2)}, u32[]{:S(2)}) async-start(bf16[64,8,640]{2,0,1:T(8,128)(2,1)} %bitcast.93), calls=%async_computation.2 | async-start | bytes 1310720 | tf_op jit(solution)/shard_map/all_to_all | solution.py:71
  54.1 30.0 %all-to-all-done.2 = bf16[64,8,640]{2,0,1:T(8,128)(2,1)S(1)} async-done(((bf16[64,8,640]{2,0,1:T(8,128)(2,1)}), bf16[64,8,640]{2,0,1:T(8,128)(2,1)S(1)}, u32[]{:S(2)}, u32[]{:S(2)}) %all-to-all-start.2) | async-done | bytes 655392 | tf_op jit(solution)/shard_map/all_to_all | solution.py:71
  84.1 7.3 %all-to-all-start = ((bf16[64,8,640]{2,0,1:T(8,128)(2,1)}), bf16[64,8,640]{2,0,1:T(8,128)(2,1)S(1)}, u32[]{:S(2)}, u32[]{:S(2)}) async-start(bf16[64,8,640]{2,0,1:T(8,128)(2,1)} %bitcast.95), calls=%async_computation | async-start | bytes 1310720 | tf_op jit(solution)/shard_map/all_to_all | solution.py:69
  93.4 28.7 %all-to-all-done = bf16[64,8,640]{2,0,1:T(8,128)(2,1)S(1)} async-done(((bf16[64,8,640]{2,0,1:T(8,128)(2,1)}), bf16[64,8,640]{2,0,1:T(8,128)(2,1)S(1)}, u32[]{:S(2)}, u32[]{:S(2)}) %all-to-all-start) | async-done | bytes 655392 | tf_op jit(solution)/shard_map/all_to_all | solution.py:69
  122.1 7.0 %all-to-all-start.3 = ((bf16[64,8,640]{2,0,1:T(8,128)(2,1)}), bf16[64,8,640]{2,0,1:T(8,128)(2,1)}, u32[]{:S(2)}, u32[]{:S(2)}) async-start(bf16[64,8,640]{2,0,1:T(8,128)(2,1)} %bitcast.92), calls=%async_computation.3 | async-start | bytes 1310720 | tf_op jit(solution)/shard_map/all_to_all | solution.py:72
  132.4 9.6 %collective-permute-start = (bf16[2,5,512,128]{3,2,1,0:T(8,128)(2,1)}, bf16[2,5,512,128]{3,2,1,0:T(8,128)(2,1)}, u32[]{:S(2)}, u32[]{:S(2)}) collective-permute-start(bf16[2,5,512,128]{3,2,1,0:T(8,128)(2,1)} %copy.90), channel_id=1, source_target_pairs={{0,8},{8,16},{16,24},{24,32},{32,40},{40,48},{48,56},{56,64},{64,7... | collective-permute-start | bytes 3932168 | tf_op jit(solution)/shard_map/ppermute | solution.py:19
  146.2 27.7 %all-to-all-done.3 = bf16[64,8,640]{2,0,1:T(8,128)(2,1)} async-done(((bf16[64,8,640]{2,0,1:T(8,128)(2,1)}), bf16[64,8,640]{2,0,1:T(8,128)(2,1)}, u32[]{:S(2)}, u32[]{:S(2)}) %all-to-all-start.3) | async-done | bytes 655392 | tf_op jit(solution)/shard_map/all_to_all | solution.py:72
  173.9 2.5 reshape.162
  178.0 27.5 %collective-permute-done = bf16[2,5,512,128]{3,2,1,0:T(8,128)(2,1)} collective-permute-done((bf16[2,5,512,128]{3,2,1,0:T(8,128)(2,1)}, bf16[2,5,512,128]{3,2,1,0:T(8,128)(2,1)}, u32[]{:S(2)}, u32[]{:S(2)}) %collective-permute-start) | collective-permute-done | bytes 1310752 | tf_op jit(solution)/shard_map/ppermute | solution.py:19
  207.7 10.4 %collective-permute-done.1 = bf16[2,5,512,128]{3,2,1,0:T(8,128)(2,1)} collective-permute-done((bf16[2,5,512,128]{3,2,1,0:T(8,128)(2,1)}, bf16[2,5,512,128]{3,2,1,0:T(8,128)(2,1)}, u32[]{:S(2)}, u32[]{:S(2)}) %collective-permute-start.1) | collective-permute-done | bytes 1310752 | tf_op jit(solution)/shard_map/ppermute | solution.py:22
  218.2 2.3 copy.93
  220.4 24.5 %pad_maximum_fusion.1 = bf16[2,5,1536,128]{3,1,2,0:T(8,128)(2,1)S(1)} fusion(bf16[2,5,512,128]{3,1,2,0:T(8,128)(2,1)S(1)} %copy.93, bf16[1,5,512,128]{3,1,2,0:T(8,128)(2,1)S(1)} %bitcast.134, bf16[1,5,512,128]{3,1,2,0:T(8,128)(2,1)S(1)} %bitcast.132, bf16[2,5,512,128]{3,1,2,0:T(8,128)(2,1)S(1)} %copy.92), kind=kLoop, calls=%fused_computation.47 | loop fusion | flops 5898240 | bytes 7864320 | tf_op jit(solution)/shard_map/concatenate | solution.py:23
  247.5 56.9 %while.19 = (s32[]{:T(128)}, bf16[5,512,128]{2,1,0:T(8,128)(2,1)}, f32[5,1536,128]{2,1,0:T(8,128)}, f32[5,1536,128]{2,1,0:T(8,128)}, bf16[5,512,128]{2,1,0:T(8,1...) while((s32[]{:T(128)}, bf16[5,512,128]{2,1,0:T(8,128)(2,1)}, ...), condition=%wide.region_5.6_spmd.clone, body=%wide.region_1.5_spmd.clone.sunk | while | flops 1219426816 | bytes 35553380 | solution.py:90
  307.6 7.7 %all-to-all-start.4 = ((bf16[8,64,640]{2,1,0:T(8,128)(2,1)}), bf16[8,64,640]{2,1,0:T(8,128)(2,1)S(1)}, u32[]{:S(2)}, u32[]{:S(2)}) async-start(bf16[8,64,640]{2,1,0:T(8,128)(2,1)} %convert_element_type.51), calls=%async_computation.4 | async-start | bytes 1310720 | tf_op jit(solution)/shard_map/all_to_all | solution.py:107
  315.3 4.1 fusion.36
  319.7 6.5 %collective-permute-start.2 = (bf16[2,5,512,128]{3,2,1,0:T(8,128)(2,1)S(1)}, bf16[2,5,512,128]{3,2,1,0:T(8,128)(2,1)S(1)}, u32[]{:S(2)}, u32[]{:S(2)}) collective-permute-start(bf16[2,5,512,128]{3,2,1,0:T(8,128)(2,1)S(1)} %get-tuple-element.183), channel_id=1, source_target_pairs={{0,8},{8,16},{16,24},{24,32},{32,40},{40,48},{48,56},{56,64},{64,7... | collective-permute-start | bytes 3932168 | tf_op jit(solution)/shard_map/ppermute | solution.py:30
  328.1 67.0 %collective-permute-done.2 = bf16[2,5,512,128]{3,2,1,0:T(8,128)(2,1)S(1)} collective-permute-done((bf16[2,5,512,128]{3,2,1,0:T(8,128)(2,1)S(1)}, bf16[2,5,512,128]{3,2,1,0:T(8,128)(2,1)S(1)}, u32[]{:S(2)}, u32[]{:S(2)}) %collective-permute-start.2) | collective-permute-done | bytes 1310752 | tf_op jit(solution)/shard_map/ppermute | solution.py:30
  395.1 17.3 %collective-permute-done.3 = bf16[2,5,512,128]{3,2,1,0:T(8,128)(2,1)S(1)} collective-permute-done((bf16[2,5,512,128]{3,2,1,0:T(8,128)(2,1)S(1)}, bf16[2,5,512,128]{3,2,1,0:T(8,128)(2,1)S(1)}, u32[]{:S(2)}, u32[]{:S(2)}) %collective-permute-start.3) | collective-permute-done | bytes 1310752 | tf_op jit(solution)/shard_map/ppermute | solution.py:30
  415.1 7.9 %all-to-all-start.5 = ((bf16[8,64,640]{2,1,0:T(8,128)(2,1)}), bf16[8,64,640]{2,1,0:T(8,128)(2,1)S(1)}, u32[]{:S(2)}, u32[]{:S(2)}) async-start(bf16[8,64,640]{2,1,0:T(8,128)(2,1)} %convert_element_type.56), calls=%async_computation.5 | async-start | bytes 1310720 | tf_op jit(solution)/shard_map/all_to_all | solution.py:108
  425.1 17.4 %all-to-all-done.5 = bf16[8,64,640]{2,1,0:T(8,128)(2,1)S(1)} async-done(((bf16[8,64,640]{2,1,0:T(8,128)(2,1)}), bf16[8,64,640]{2,1,0:T(8,128)(2,1)S(1)}, u32[]{:S(2)}, u32[]{:S(2)}) %all-to-all-start.5) | async-done | bytes 655392 | tf_op jit(solution)/shard_map/all_to_all | solution.py:108
  442.4 5.1 %all-to-all-start.6 = ((bf16[8,64,640]{2,1,0:T(8,128)(2,1)}), bf16[8,64,640]{2,1,0:T(8,128)(2,1)S(1)}, u32[]{:S(2)}, u32[]{:S(2)}) async-start(bf16[8,64,640]{2,1,0:T(8,128)(2,1)} %convert_element_type.59), calls=%async_computation.6 | async-start | bytes 1310720 | tf_op jit(solution)/shard_map/all_to_all | solution.py:109
  449.3 17.7 %all-to-all-done.6 = bf16[8,64,640]{2,1,0:T(8,128)(2,1)S(1)} async-done(((bf16[8,64,640]{2,1,0:T(8,128)(2,1)}), bf16[8,64,640]{2,1,0:T(8,128)(2,1)S(1)}, u32[]{:S(2)}, u32[]{:S(2)}) %all-to-all-start.6) | async-done | bytes 655392 | tf_op jit(solution)/shard_map/all_to_all | solution.py:109
  (106 shorter events, 90.2 us)
Async XLA Ops:
  0.6 143.3 %copy-start = (s32[512,16]{0,1:T(8,128)S(1)}, s32[512,16]{0,1:T(8,128)}, u32[]{:S(2)}) copy-start(s32[512,16]{0,1:T(8,128)} %param.20) | copy-start | bytes 98308
  0.6 52.6 %copy-start.6 = (bf16[64,5120]{1,0:T(8,128)(2,1)S(1)}, bf16[64,5120]{1,0:T(8,128)(2,1)}, u32[]{:S(2)}) copy-start(bf16[64,5120]{1,0:T(8,128)(2,1)} %param.16) | copy-start | bytes 1966084
  2.7 43.2 %all-to-all-start.1 = ((bf16[64,8,640]{2,0,1:T(8,128)(2,1)}), bf16[64,8,640]{2,0,1:T(8,128)(2,1)S(1)}, u32[]{:S(2)}, u32[]{:S(2)}) async-start(bf16[64,8,640]{2,0,1:T(8,128)(2,1)} %bitcast.94), calls=%async_computation.1 | async-start | bytes 1310720 | tf_op jit(solution)/shard_map/all_to_all | solution.py:70
  45.9 38.2 %all-to-all-start.2 = ((bf16[64,8,640]{2,0,1:T(8,128)(2,1)}), bf16[64,8,640]{2,0,1:T(8,128)(2,1)S(1)}, u32[]{:S(2)}, u32[]{:S(2)}) async-start(bf16[64,8,640]{2,0,1:T(8,128)(2,1)} %bitcast.93), calls=%async_computation.2 | async-start | bytes 1310720 | tf_op jit(solution)/shard_map/all_to_all | solution.py:71
  84.1 38.0 %all-to-all-start = ((bf16[64,8,640]{2,0,1:T(8,128)(2,1)}), bf16[64,8,640]{2,0,1:T(8,128)(2,1)S(1)}, u32[]{:S(2)}, u32[]{:S(2)}) async-start(bf16[64,8,640]{2,0,1:T(8,128)(2,1)} %bitcast.95), calls=%async_computation | async-start | bytes 1310720 | tf_op jit(solution)/shard_map/all_to_all | solution.py:69
  122.1 51.8 %all-to-all-start.3 = ((bf16[64,8,640]{2,0,1:T(8,128)(2,1)}), bf16[64,8,640]{2,0,1:T(8,128)(2,1)}, u32[]{:S(2)}, u32[]{:S(2)}) async-start(bf16[64,8,640]{2,0,1:T(8,128)(2,1)} %bitcast.92), calls=%async_computation.3 | async-start | bytes 1310720 | tf_op jit(solution)/shard_map/all_to_all | solution.py:72
  130.5 1.9 copy-start.4
  132.4 73.1 %collective-permute-start = (bf16[2,5,512,128]{3,2,1,0:T(8,128)(2,1)}, bf16[2,5,512,128]{3,2,1,0:T(8,128)(2,1)}, u32[]{:S(2)}, u32[]{:S(2)}) collective-permute-start(bf16[2,5,512,128]{3,2,1,0:T(8,128)(2,1)} %copy.90), channel_id=1, source_target_pairs={{0,8},{8,16},{16,24},{24,32},{32,40},{40,48},{48,56},{56,64},{64,7... | collective-permute-start | bytes 3932168 | tf_op jit(solution)/shard_map/ppermute | solution.py:19
  142.0 76.2 %collective-permute-start.1 = (bf16[2,5,512,128]{3,2,1,0:T(8,128)(2,1)}, bf16[2,5,512,128]{3,2,1,0:T(8,128)(2,1)}, u32[]{:S(2)}, u32[]{:S(2)}) collective-permute-start(bf16[2,5,512,128]{3,2,1,0:T(8,128)(2,1)} %copy.90), channel_id=1, source_target_pairs={{8,0},{16,8},{24,16},{32,24},{40,32},{48,40},{56,48},{64,56},{72,6... | collective-permute-start | bytes 3932168 | tf_op jit(solution)/shard_map/ppermute | solution.py:22
  178.0 42.4 %copy-start.5 = (bf16[512,5,128]{2,1,0:T(8,128)(2,1)S(1)}, bf16[512,5,128]{2,1,0:T(8,128)(2,1)}, u32[]{:S(2)}) copy-start(bf16[512,5,128]{2,1,0:T(8,128)(2,1)} %copy-done.4) | copy-start | bytes 1966084
  307.6 107.5 %all-to-all-start.4 = ((bf16[8,64,640]{2,1,0:T(8,128)(2,1)}), bf16[8,64,640]{2,1,0:T(8,128)(2,1)S(1)}, u32[]{:S(2)}, u32[]{:S(2)}) async-start(bf16[8,64,640]{2,1,0:T(8,128)(2,1)} %convert_element_type.51), calls=%async_computation.4 | async-start | bytes 1310720 | tf_op jit(solution)/shard_map/all_to_all | solution.py:107
  315.3 97.1 %copy-start.3 = (f32[5,1536,128]{2,1,0:T(8,128)S(1)}, f32[5,1536,128]{2,1,0:T(8,128)}, u32[]{:S(2)}) copy-start(f32[5,1536,128]{2,1,0:T(8,128)} %get-tuple-element.94) | copy-start | bytes 11796484
  319.4 93.0 %copy-start.2 = (f32[5,1536,128]{2,1,0:T(8,128)S(1)}, f32[5,1536,128]{2,1,0:T(8,128)}, u32[]{:S(2)}) copy-start(f32[5,1536,128]{2,1,0:T(8,128)} %get-tuple-element.93) | copy-start | bytes 11796484
  319.7 75.4 %collective-permute-start.2 = (bf16[2,5,512,128]{3,2,1,0:T(8,128)(2,1)S(1)}, bf16[2,5,512,128]{3,2,1,0:T(8,128)(2,1)S(1)}, u32[]{:S(2)}, u32[]{:S(2)}) collective-permute-start(bf16[2,5,512,128]{3,2,1,0:T(8,128)(2,1)S(1)} %get-tuple-element.183), channel_id=1, source_target_pairs={{0,8},{8,16},{16,24},{24,32},{32,40},{40,48},{48,56},{56,64},{64,7... | collective-permute-start | bytes 3932168 | tf_op jit(solution)/shard_map/ppermute | solution.py:30
  326.1 86.3 %collective-permute-start.3 = (bf16[2,5,512,128]{3,2,1,0:T(8,128)(2,1)S(1)}, bf16[2,5,512,128]{3,2,1,0:T(8,128)(2,1)S(1)}, u32[]{:S(2)}, u32[]{:S(2)}) collective-permute-start(bf16[2,5,512,128]{3,2,1,0:T(8,128)(2,1)S(1)} %get-tuple-element.184), channel_id=1, source_target_pairs={{8,0},{16,8},{24,16},{32,24},{40,32},{48,40},{56,48},{64,56},{72,6... | collective-permute-start | bytes 3932168 | tf_op jit(solution)/shard_map/ppermute | solution.py:30
  415.1 27.3 %all-to-all-start.5 = ((bf16[8,64,640]{2,1,0:T(8,128)(2,1)}), bf16[8,64,640]{2,1,0:T(8,128)(2,1)S(1)}, u32[]{:S(2)}, u32[]{:S(2)}) async-start(bf16[8,64,640]{2,1,0:T(8,128)(2,1)} %convert_element_type.56), calls=%async_computation.5 | async-start | bytes 1310720 | tf_op jit(solution)/shard_map/all_to_all | solution.py:108
  423.0 44.9 %copy-start.1 = (s32[512,16]{0,1:T(8,128)S(1)}, s32[512,16]{0,1:T(8,128)}, u32[]{:S(2)}) copy-start(s32[512,16]{0,1:T(8,128)} %param.20) | copy-start | bytes 98308
  442.4 24.5 %all-to-all-start.6 = ((bf16[8,64,640]{2,1,0:T(8,128)(2,1)}), bf16[8,64,640]{2,1,0:T(8,128)(2,1)S(1)}, u32[]{:S(2)}, u32[]{:S(2)}) async-start(bf16[8,64,640]{2,1,0:T(8,128)(2,1)} %convert_element_type.59), calls=%async_computation.6 | async-start | bytes 1310720 | tf_op jit(solution)/shard_map/all_to_all | solution.py:109
where the time goes:
time: 469 us; the launch traced here: 468 us
  waiting for transfers between devices  273 us (58%)
  starting transfers between devices  74.2 us (16%)
  matrix products  42.2 us (9%)
  local copies, waits for them, and re-layouts  38.8 us (8%)
  other arithmetic  38.8 us (8%)
    ppermute x2, waiting for transfers between devices, passed_along(): return lax.ppermute(array, axis, pairs)  84.4 us
    all_to_all x1, waiting for transfers between devices, per_device(): lax.all_to_all(values, 'head', split_axis=1, concat_axis=0, tiled=True)  30 us
    all_to_all x1, waiting for transfers between devices, per_device(): lax.all_to_all(keys, 'head', split_axis=1, concat_axis=0, tiled=True)  29.1 us
    all_to_all x1, waiting for transfers between devices, per_device(): lax.all_to_all(queries, 'head', split_axis=1, concat_axis=0, tiled=True)  28.7 us
    all_to_all x1, waiting for transfers between devices, per_device(): lax.all_to_all(grad_out, 'head', split_axis=1, concat_axis=0, tiled=True)  27.7 us
    ppermute x1, waiting for transfers between devices, extended(): lax.ppermute(lax.slice_in_dim(block, block.shape[dim] - width, None, axis...  27.5 us
    concatenate x1, other arithmetic, extended(): block = jnp.concatenate([low, block, high], axis=dim)  24.5 us
    all_to_all x1, waiting for transfers between devices, per_device(): lax.all_to_all(grad_v_rows, 'head', split_axis=0, concat_axis=1, tiled=True)  17.7 us
  transfers between devices with their start and end apart: 11, of which 10 were waited for; matrix products, arithmetic and copies ran while one was open for 6% of the time, Pallas kernels for 0%

commit v1 on v0

v1 whole, which is shorter than its diff:
```python
import functools
import math

import jax
import jax.numpy as jnp
from jax import lax
from jax.experimental import pallas as pl
from jax.experimental.pallas import tpu as pltpu
from jax.sharding import PartitionSpec as P

DH = 128
TILE = 64
MESH = pl.DeviceIdType.MESH
AHEAD = 2


def wait_bytes(ref, sem):
    pltpu.make_async_copy(ref, ref, sem).wait()


def kernel(
    slabs, width, head_count, block,
    q_in, k_in, v_in, d_in, listed,
    dq_out, dk_out, dv_out,
    q_rows, d_rows, k_win, v_win, bias, acc_k, acc_v, own, part_out, part_in, stage,
    in_send, in_recv, halo_send, halo_recv, part_send, part_recv, out_send, out_recv,
):
    slab = lax.axis_index("ctx")
    place = lax.axis_index("head")
    rows = width * TILE
    above, below = (slab + 1) % slabs, (slab + slabs - 1) % slabs

    def flipped(index):
        return index // (slabs // 2)

    def group_at(where):
        return where + flipped(slab) * (width - 1 - 2 * where)

    def beside(other):
        crossing = (flipped(slab) + flipped(other)) % 2
        return (other, place + crossing * (width - 1 - 2 * place))

    group = group_at(place)
    near = (beside(below), beside(above))
    steps = sorted(range(1, width), key=lambda j: (abs(j - width // 2), j))
    scale = 1.0 / math.sqrt(DH)

    barrier = pltpu.get_barrier_semaphore()
    for j in steps:
        pl.semaphore_signal(
            barrier, inc=1, device_id=(slab, (place + j) % width), device_id_type=MESH
        )
    for target in near:
        pl.semaphore_signal(barrier, inc=1, device_id=target, device_id_type=MESH)
    pl.semaphore_wait(barrier, width + 1)

    def head_columns(which, head):
        return pl.ds(pl.multiple_of((which * head_count + head) * DH, DH), DH)

    own_rows = pl.ds(rows + pl.multiple_of(place * TILE, TILE), TILE)
    slab_rows = pl.ds(pl.multiple_of(place * TILE, TILE), TILE)
    inputs = (
        (k_in, k_win, own_rows), (v_in, v_win, own_rows),
        (q_in, q_rows, slab_rows), (d_in, d_rows, slab_rows),
    )

    def send_inputs(head):
        for i, (source, target, where) in enumerate(inputs):
            for j in steps:
                other = (place + j) % width
                pltpu.make_async_remote_copy(
                    src_ref=source.at[:, head_columns(group_at(other), head)],
                    dst_ref=target.at[head, where],
                    send_sem=in_send.at[i],
                    recv_sem=in_recv.at[i, head],
                    device_id=(slab, other),
                    device_id_type=MESH,
                ).start()
            pltpu.make_async_copy(
                source.at[:, head_columns(group, head)],
                target.at[head, where],
                in_recv.at[i, head],
            ).start()

    def send_halo(head):
        for i, window in enumerate((k_win, v_win)):
            for side in range(2):
                pltpu.make_async_remote_copy(
                    src_ref=window.at[head, pl.ds(rows, rows)],
                    dst_ref=window.at[head, pl.ds(2 * rows * (1 - side), rows)],
                    send_sem=halo_send.at[i, side],
                    recv_sem=halo_recv.at[i, 1 - side, head],
                    device_id=near[side],
                    device_id_type=MESH,
                ).start()

    def send_result(index, head, target):
        for j in steps:
            other = (place + j) % width
            pltpu.make_async_remote_copy(
                src_ref=stage.at[index, head, pl.ds(pl.multiple_of(other * TILE, TILE), TILE)],
                dst_ref=target.at[:, head_columns(group, head)],
                send_sem=out_send.at[index],
                recv_sem=out_recv.at[index],
                device_id=(slab, other),
                device_id_type=MESH,
            ).start()
        pltpu.make_async_copy(
            stage.at[index, head, slab_rows],
            target.at[:, head_columns(group, head)],
            out_recv.at[index],
        ).start()

    def attend(head):
        acc_k[...] = jnp.zeros_like(acc_k)
        acc_v[...] = jnp.zeros_like(acc_v)

        @pl.loop(0, rows // block)
        def _(step):
            start = pl.multiple_of(step * block, block)
            picked = pl.ds(start, block)
            query, cotan = q_rows[head, picked], d_rows[head, picked]
            key, value = k_win[head], v_win[head]
            last = (((1,), (1,)), ((), ()))
            first = (((0,), (0,)), ((), ()))
            scores = lax.dot_general(key, query, last, preferred_element_type=jnp.float32)
            scores = scores.reshape(3 * width, TILE, block) * (scale / math.log(2.0))
            scores = (scores + bias[:, picked][:, None, :]).reshape(3 * rows, block)
            expo = jnp.exp2(scores - jnp.max(scores, axis=0, keepdims=True))
            probs = expo * (1.0 / jnp.sum(expo, axis=0, keepdims=True))
            grad_p = lax.dot_general(value, cotan, last, preferred_element_type=jnp.float32)
            delta = jnp.sum(probs * grad_p, axis=0, keepdims=True)
            grad_s = (probs * (grad_p - delta)).astype(jnp.bfloat16)
            acc_v[...] += jnp.dot(
                probs.astype(jnp.bfloat16), cotan, preferred_element_type=jnp.float32
            )
            acc_k[...] += jnp.dot(grad_s, query, preferred_element_type=jnp.float32)
            grad_q = lax.dot_general(grad_s, key, first, preferred_element_type=jnp.float32)
            stage[0, head, picked] = (grad_q * scale).astype(jnp.bfloat16)

        for i, (acc, factor) in enumerate(((acc_k, scale), (acc_v, 1.0))):
            own[i, head] = acc[rows : 2 * rows] * factor
            part_out[0, i, head] = (acc[:rows] * factor).astype(jnp.bfloat16)
            part_out[1, i, head] = (acc[2 * rows :] * factor).astype(jnp.bfloat16)

    def send_parts(head):
        for i in range(2):
            for side in range(2):
                pltpu.make_async_remote_copy(
                    src_ref=part_out.at[side, i, head],
                    dst_ref=part_in.at[1 - side, i, head],
                    send_sem=part_send.at[i, side],
                    recv_sem=part_recv.at[i, 1 - side, head],
                    device_id=near[side],
                    device_id_type=MESH,
                ).start()

    def finish(head):
        for i, target in enumerate((dk_out, dv_out)):
            for side in range(2):
                wait_bytes(part_in.at[side, i, head], part_recv.at[i, side, head])
            total = (
                own[i, head]
                + part_in[0, i, head].astype(jnp.float32)
                + part_in[1, i, head].astype(jnp.float32)
            )
            stage[1 + i, head] = total.astype(jnp.bfloat16)
            send_result(1 + i, head, target)

    for head in range(min(AHEAD, head_count)):
        send_inputs(head)

    tiles = lax.broadcasted_iota(jnp.int32, bias.shape, 0)
    hit = tiles == listed[0:1, :]
    for n in range(1, listed.shape[0]):
        hit = hit | (tiles == listed[n : n + 1, :])
    bias[...] = jnp.where(hit, 0.0, -1e30)

    @pl.loop(0, head_count)
    def _(head):
        for i, window in enumerate((k_win, v_win)):
            wait_bytes(window.at[head, pl.ds(rows, rows)], in_recv.at[i, head])
        send_halo(head)

        @pl.when(head + AHEAD < head_count)
        def _():
            send_inputs(head + AHEAD)

        wait_bytes(q_rows.at[head], in_recv.at[2, head])
        wait_bytes(d_rows.at[head], in_recv.at[3, head])
        for i, window in enumerate((k_win, v_win)):
            for side in range(2):
                wait_bytes(
                    window.at[head, pl.ds(2 * rows * side, rows)], halo_recv.at[i, side, head]
                )
        attend(head)
        send_parts(head)
        send_result(0, head, dq_out)

        @pl.when(head >= 1)
        def _():
            finish(head - 1)

    finish(head_count - 1)

    remote = pl.ds(0, rows - TILE)
    for i in range(4):
        wait_bytes(k_win.at[:, remote], in_send.at[i])
    for i in range(2):
        for side in range(2):
            wait_bytes(q_rows, halo_send.at[i, side])
            wait_bytes(q_rows, part_send.at[i, side])
    for i, target in enumerate((dq_out, dk_out, dv_out)):
        wait_bytes(stage.at[i, :, remote], out_send.at[i])
        wait_bytes(target, out_recv.at[i])


def per_device(slabs, width, queries, keys, values, grad_out, neighbours, counts):
    tile_rows, features = queries.shape
    head_count = features // DH // width
    rows = width * TILE
    first = lax.axis_index("ctx") * width
    own_nbr = lax.dynamic_slice_in_dim(neighbours, first, width, 0)
    own_cnt = lax.dynamic_slice_in_dim(counts, first, width, 0)
    used = lax.broadcasted_iota(jnp.int32, own_nbr.shape, 1) < own_cnt[:, None]
    listed = jnp.repeat(jnp.where(used, own_nbr - first + width, -1).T, TILE, axis=1)
    block = min(256, rows)
    whole = pl.BlockSpec(memory_space=pl.ANY)
    half = jnp.bfloat16
    dma = pltpu.SemaphoreType.DMA
    flops = 5 * 2 * rows * 3 * rows * DH * head_count
    return pl.pallas_call(
        functools.partial(kernel, slabs, width, head_count, block),
        out_shape=[jax.ShapeDtypeStruct((tile_rows, features), half)] * 3,
        in_specs=[whole] * 4 + [pl.BlockSpec(memory_space=pltpu.VMEM)],
        out_specs=[whole] * 3,
        scratch_shapes=[
            pltpu.VMEM((head_count, rows, DH), half),
            pltpu.VMEM((head_count, rows, DH), half),
            pltpu.VMEM((head_count, 3 * rows, DH), half),
            pltpu.VMEM((head_count, 3 * rows, DH), half),
            pltpu.VMEM((3 * width, rows), jnp.float32),
            pltpu.VMEM((3 * rows, DH), jnp.float32),
            pltpu.VMEM((3 * rows, DH), jnp.float32),
            pltpu.VMEM((2, head_count, rows, DH), jnp.float32),
            pltpu.VMEM((2, 2, head_count, rows, DH), half),
            pltpu.VMEM((2, 2, head_count, rows, DH), half),
            pltpu.VMEM((3, head_count, rows, DH), half),
            dma((4,)),
            dma((4, head_count)),
            dma((2, 2)),
            dma((2, 2, head_count)),
            dma((2, 2)),
            dma((2, 2, head_count)),
            dma((3,)),
            dma((3,)),
        ],
        compiler_params=pltpu.CompilerParams(
            collective_id=0, has_side_effects=True, vmem_limit_bytes=56 * 1024 * 1024
        ),
        cost_estimate=pl.CostEstimate(
            flops=flops, bytes_accessed=7 * tile_rows * features * 2, transcendentals=0
        ),
    )(queries, keys, values, grad_out, listed)


def solution(mesh):
    split = P(("ctx", "head"), None)
    return jax.shard_map(
        functools.partial(per_device, mesh.shape["ctx"], mesh.shape["head"]),
        mesh=mesh,
        in_specs=(split, split, split, split, P(), P()),
        out_specs=(split, split, split),
        check_vma=False,
    )
```

time: 469 us -> 263 us (0.56)
  the two profiles are of different devices: /device:TPU:63 before, /device:TPU:32 now
where the time goes in v1:
time: 263 us
  Pallas kernels  256 us (97%)
  local copies, waits for them, and re-layouts  5.73 us (2%)
    pallas_call x1, Pallas kernels, per_device(): pl.pallas_call(functools.partial(kernel, slabs, width, head_count, block)...  256 us

profile of v1, /device:TPU:32, one launch (start us, length us, event | category | flops | bytes accessed | tf_op | source)
XLA Modules:
  0.0 262.9 jit_solution(3043163480935473315)
XLA Ops:
  0.6 0.8 dynamic_slice.6
  1.4 0.8 select_bitcast_fusion
  2.2 0.1 broadcast_in_dim.9
  2.2 0.7 reshape.10.listed
  2.9 255.8 %shard_map.85 = (bf16[64,5120]{1,0:T(8,128)(2,1)}, bf16[64,5120]{1,0:T(8,128)(2,1)}, bf16[64,5120]{1,0:T(8,128)(2,1)}) custom-call(bf16[64,5120]{1,0:T(8,128)(2,1)} %q_in.1, bf16[64,5120]{1,0:T(8,128)(2,1)} %k_in.1, bf16[64,5120]{1,0:T(8,128)(2,1)} %v_in.1, bf16[64,5120]{1,0:T(8,128)(2,1)} %d_in.1, s32[16,512]{1,0:T(8,128)} %reshape.10.listed), custom_call_target="tpu_custom_call" | custom-call | flops 5033164800 | bytes 4587520 | tf_op jit(solution)/shard_map/pallas_call | solution.py:232
  258.7 0.0 copy-start.1
  258.7 2.0 copy.12
  260.8 0.0 copy-done.1
  260.8 0.0 copy-start
  260.8 0.8 copy.13
  261.6 0.5 copy-done
  262.1 0.8 copy.14
Async XLA Ops:
  258.7 2.0 copy-start.1
  260.8 1.3 copy-start

commit v2 on v1

--- a/solution.py
+++ b/solution.py
@@ -20,9 +20,9 @@
 
 def kernel(
     slabs, width, head_count, block,
-    q_in, k_in, v_in, d_in, listed,
+    q_in, k_in, v_in, d_in, neighbours, counts,
     dq_out, dk_out, dv_out,
-    q_rows, d_rows, k_win, v_win, bias, acc_k, acc_v, own, part_out, part_in, stage,
+    q_rows, d_rows, k_win, v_win, listed, bias, acc_k, acc_v, own, part_out, part_in, stage, list_sem,
     in_send, in_recv, halo_send, halo_recv, part_send, part_recv, out_send, out_recv,
 ):
     slab = lax.axis_index("ctx")
@@ -44,6 +44,11 @@
     near = (beside(below), beside(above))
     steps = sorted(range(1, width), key=lambda j: (abs(j - width // 2), j))
     scale = 1.0 / math.sqrt(DH)
+
+    lists = pltpu.make_async_copy(
+        neighbours.at[pl.ds(pl.multiple_of(slab * width, width), width)], listed, list_sem
+    )
+    lists.start()
 
     barrier = pltpu.get_barrier_semaphore()
     for j in steps:
@@ -59,13 +64,11 @@
 
     own_rows = pl.ds(rows + pl.multiple_of(place * TILE, TILE), TILE)
     slab_rows = pl.ds(pl.multiple_of(place * TILE, TILE), TILE)
-    inputs = (
-        (k_in, k_win, own_rows), (v_in, v_win, own_rows),
-        (q_in, q_rows, slab_rows), (d_in, d_rows, slab_rows),
-    )
-
-    def send_inputs(head):
-        for i, (source, target, where) in enumerate(inputs):
+    pair_kv = ((0, k_in, k_win, own_rows), (1, v_in, v_win, own_rows))
+    pair_qd = ((2, q_in, q_rows, slab_rows), (3, d_in, d_rows, slab_rows))
+
+    def send_inputs(pair, head):
+        for i, source, target, where in pair:
             for j in steps:
                 other = (place + j) % width
                 pltpu.make_async_remote_copy(
@@ -167,14 +170,18 @@
             stage[1 + i, head] = total.astype(jnp.bfloat16)
             send_result(1 + i, head, target)
 
-    for head in range(min(AHEAD, head_count)):
-        send_inputs(head)
-
-    tiles = lax.broadcasted_iota(jnp.int32, bias.shape, 0)
-    hit = tiles == listed[0:1, :]
-    for n in range(1, listed.shape[0]):
-        hit = hit | (tiles == listed[n : n + 1, :])
-    bias[...] = jnp.where(hit, 0.0, -1e30)
+    for head in range(AHEAD):
+        send_inputs(pair_kv, head)
+
+    lists.wait()
+    tiles = lax.broadcasted_iota(jnp.int32, (3 * width, TILE), 0)
+    first = (slab - 1) * width
+    for t in range(width):
+        hit = tiles < 0
+        for n in range(listed.shape[1]):
+            used = n < counts[slab * width + t]
+            hit = hit | (tiles == jnp.where(used, listed[t, n] - first, -1))
+        bias[:, t * TILE : (t + 1) * TILE] = jnp.where(hit, 0.0, -1e30)
 
     @pl.loop(0, head_count)
     def _(head):
@@ -184,10 +191,21 @@
 
         @pl.when(head + AHEAD < head_count)
         def _():
-            send_inputs(head + AHEAD)
-
+            send_inputs(pair_kv, head + AHEAD)
+
+        @pl.when(head + AHEAD >= head_count)
+        def _():
+            send_inputs(pair_qd, head + AHEAD - head_count)
+
+    @pl.loop(0, head_count)
+    def _(head):
         wait_bytes(q_rows.at[head], in_recv.at[2, head])
         wait_bytes(d_rows.at[head], in_recv.at[3, head])
+
+        @pl.when(head + AHEAD < head_count)
+        def _():
+            send_inputs(pair_qd, head + AHEAD)
+
         for i, window in enumerate((k_win, v_win)):
             for side in range(2):
                 wait_bytes(
@@ -197,11 +215,9 @@
         send_parts(head)
         send_result(0, head, dq_out)
 
-        @pl.when(head >= 1)
-        def _():
-            finish(head - 1)
-
-    finish(head_count - 1)
+    @pl.loop(0, head_count)
+    def _(head):
+        finish(head)
 
     remote = pl.ds(0, rows - TILE)
     for i in range(4):
@@ -219,12 +235,7 @@
     tile_rows, features = queries.shape
     head_count = features // DH // width
     rows = width * TILE
-    first = lax.axis_index("ctx") * width
-    own_nbr = lax.dynamic_slice_in_dim(neighbours, first, width, 0)
-    own_cnt = lax.dynamic_slice_in_dim(counts, first, width, 0)
-    used = lax.broadcasted_iota(jnp.int32, own_nbr.shape, 1) < own_cnt[:, None]
-    listed = jnp.repeat(jnp.where(used, own_nbr - first + width, -1).T, TILE, axis=1)
-    block = min(256, rows)
+    block = min(512, rows)
     whole = pl.BlockSpec(memory_space=pl.ANY)
     half = jnp.bfloat16
     dma = pltpu.SemaphoreType.DMA
@@ -232,13 +243,14 @@
     return pl.pallas_call(
         functools.partial(kernel, slabs, width, head_count, block),
         out_shape=[jax.ShapeDtypeStruct((tile_rows, features), half)] * 3,
-        in_specs=[whole] * 4 + [pl.BlockSpec(memory_space=pltpu.VMEM)],
+        in_specs=[whole] * 5 + [pl.BlockSpec(memory_space=pltpu.SMEM)],
         out_specs=[whole] * 3,
         scratch_shapes=[
             pltpu.VMEM((head_count, rows, DH), half),
             pltpu.VMEM((head_count, rows, DH), half),
             pltpu.VMEM((head_count, 3 * rows, DH), half),
             pltpu.VMEM((head_count, 3 * rows, DH), half),
+            pltpu.SMEM((width, neighbours.shape[1]), jnp.int32),
             pltpu.VMEM((3 * width, rows), jnp.float32),
             pltpu.VMEM((3 * rows, DH), jnp.float32),
             pltpu.VMEM((3 * rows, DH), jnp.float32),
@@ -246,6 +258,7 @@
             pltpu.VMEM((2, 2, head_count, rows, DH), half),
             pltpu.VMEM((2, 2, head_count, rows, DH), half),
             pltpu.VMEM((3, head_count, rows, DH), half),
+            dma(()),
             dma((4,)),
             dma((4, head_count)),
             dma((2, 2)),
@@ -261,7 +274,7 @@
         cost_estimate=pl.CostEstimate(
             flops=flops, bytes_accessed=7 * tile_rows * features * 2, transcendentals=0
         ),
-    )(queries, keys, values, grad_out, listed)
+    )(queries, keys, values, grad_out, neighbours, counts)
 
 
 def solution(mesh):

time: 263 us -> 243 us (0.924)
  the two profiles are of different devices: /device:TPU:32 before, /device:TPU:31 now
where the time goes in v2:
time: 243 us; the launch traced here: 242 us
  Pallas kernels  236 us (97%)
  local copies, waits for them, and re-layouts  5.79 us (2%)
    pallas_call x1, Pallas kernels, per_device(): pl.pallas_call(functools.partial(kernel, slabs, width, head_count, block)...  236 us
    unnamed x8, local copies, waits for them, and re-layouts  5.79 us

profile of v2, /device:TPU:31, one launch (start us, length us, event | category | flops | bytes accessed | tf_op | source)
XLA Modules:
  0.0 242.4 jit_solution(17606475854069432789)
XLA Ops:
  0.6 1.6 copy.9.neighbours
  2.2 235.9 %shard_map.85 = (bf16[64,5120]{1,0:T(8,128)(2,1)}, bf16[64,5120]{1,0:T(8,128)(2,1)}, bf16[64,5120]{1,0:T(8,128)(2,1)}) custom-call(bf16[64,5120]{1,0:T(8,128)(2,1)} %q_in.1, bf16[64,5120]{1,0:T(8,128)(2,1)} %k_in.1, bf16[64,5120]{1,0:T(8,128)(2,1)} %v_in.1, bf16[64,5120]{1,0:T(8,128)(2,1)} %d_in.1, s32[512,16]{1,0:T(8,128)} %copy.9.neighbours, s32[512]{0:T(512)} %counts.1), custom_call_target="tpu_custom_call" | custom-call | flops 5033164800 | bytes 4587520 | tf_op jit(solution)/shard_map/pallas_call | solution.py:243
  238.2 0.0 copy-start.1
  238.2 2.0 copy.13
  240.2 0.0 copy-done.1
  240.2 0.0 copy-start
  240.2 0.8 copy.14
  241.0 0.5 copy-done
  241.5 0.8 copy.15
Async XLA Ops:
  238.2 2.0 copy-start.1
  240.2 1.3 copy-start
